TPU v7x, 32 devices: a whole 2x2x4 slice. The times are simulated.
32 devices in a mesh: chan: 16 (over z, y, x), pos: 2 (over core).
Axes of the slice: x: 2, y: 2, z: 4, core: 2. Of those that a mesh axis runs over, the one named last changes fastest.
Arguments:
- patches: bfloat16 [16, 2, 512, 256], P(None, 'pos', 'chan'), may hold values from -30 to 30
- tok_weight: bfloat16 [32, 256, 1024], P('chan'), may hold values from -2 to 2
- mixing: bfloat16 [32, 16, 16], P('chan'), may hold values from -1.5 to 1.5
- chan_embed: bfloat16 [512, 1024], P('chan'), may hold values from -3 to 3
- norm_gain: float32 [1024], replicated, may hold values from 0.5 to 1.5
- qkv_weight: bfloat16 [1024, 3072], replicated, may hold values from -8 to 8
- upstream: bfloat16 [16, 2, 512, 1024], P(None, 'pos', 'chan'), may hold values from -6 to 6
Outputs:
- encoded: bfloat16 [16, 2, 512, 1024], P(None, 'pos', 'chan')
- tok_grad: float32 [2, 32, 256, 1024], P('pos', 'chan')
- mix_grad: float32 [32, 16, 16], P('chan')
- embed_grad: float32 [512, 1024], P('chan')
All inputs are finite; a program needn't handle non-finite values.
Results may differ from a plain program's by a relative error of at most 0.006.
The roundings to bfloat16 on the way count: a program that leaves them out, or rounds other values in their place, can miss the bound.
Values may be sent and summed in bfloat16 or wider, within the bound.
A program may use at most 128 MiB of HBM per device.

v0:
```python
import functools
import math

import jax
import jax.numpy as jnp
from jax import lax
from jax.experimental import pallas as pl
from jax.experimental.pallas import tpu as pltpu
from jax.sharding import PartitionSpec as P

HDIM = 128
F32 = jnp.float32
BF16 = jnp.bfloat16
HIGH = lax.Precision.HIGHEST


def dot(a, b, ca=1, cb=0):
    return lax.dot_general(a, b, (((ca,), (cb,)), ((), ())), preferred_element_type=F32)


def kernel(
    n, npos,
    patches, tokw, mixing, embed, gain, w_hbm, up_hbm,
    enc_out, tok_out, mix_out, emb_out,
    tokens, mixed, mixp, upp, upl, w, proj, probs, inv, encs, gproj, gn, gbs, gbr,
    emb_all, mix_all, gtok, emb_up,
    s1, r1, s2, r2, s3, r3, s4, r4, se, re, sm, rm, lsem,
):
    me = lax.axis_index("chan")
    mypos = lax.axis_index("pos")
    rows, _, cc, pix = patches.shape
    groups, group, _ = mixing.shape
    width = embed.shape[1]
    chans = n * cc
    heads = width // HDIM

    barrier = pltpu.get_barrier_semaphore()

    def greet(d, c):
        pl.semaphore_signal(barrier, inc=1, device_id={"chan": lax.rem(me + d, n)})
        return c

    lax.fori_loop(1, n, greet, 0)

    def greet_pos(q, c):
        pl.semaphore_signal(barrier, inc=1, device_id={"pos": lax.rem(mypos + q, npos)})
        return c

    lax.fori_loop(1, npos, greet_pos, 0)

    w_copy = pltpu.make_async_copy(w_hbm, w, lsem.at[0])
    up_copy = pltpu.make_async_copy(up_hbm.at[:, 0], upl, lsem.at[1])
    own_up = pltpu.make_async_copy(up_hbm.at[me, 0], upp.at[me], lsem.at[2])
    up_copy.start()
    own_up.start()
    w_copy.start()

    def remote(src, dst, ss, rs, d, peer):
        return pltpu.make_async_remote_copy(
            src_ref=src, dst_ref=dst, send_sem=ss.at[d], recv_sem=rs.at[d], device_id={"chan": peer}
        )

    long = rows * group
    pick = (lax.broadcasted_iota(jnp.int32, (long, group), 0) % group
            == lax.broadcasted_iota(jnp.int32, (long, group), 1))
    pick_f = pick.astype(F32)
    same = (lax.broadcasted_iota(jnp.int32, (long, long), 0) // group
            == lax.broadcasted_iota(jnp.int32, (long, long), 1) // group)

    def block_diag(g):
        tall = dot(pick_f.astype(BF16), mixing[g]).astype(BF16)
        full = dot(tall, pick_f.astype(BF16), 1, 1)
        return jnp.where(same, full, 0.0).astype(BF16)

    for g in range(groups):
        ch = slice(g * group, (g + 1) * group)
        pg = patches[:, 0, ch, :].reshape(long, pix)
        tok = dot(pg, tokw[g]).astype(BF16)
        tokens[g] = tok
        mix = dot(block_diag(g), tok).reshape(rows, group, width) + embed[ch, :].astype(F32)[None]
        mixed[:, ch, :] = mix.astype(BF16)

    pl.semaphore_wait(barrier, n - 1 + npos - 1)

    def send1(d, c):
        peer = lax.rem(me + d, n)
        remote(mixed.at[peer], mixp.at[me], s1, r1, d, peer).start()
        return c

    lax.fori_loop(1, n, send1, 0)

    def send2(d, c):
        peer = lax.rem(me + d, n)
        remote(up_hbm.at[peer, 0], upp.at[me], s2, r2, d, peer).start()
        return c

    lax.fori_loop(1, n, send2, 0)

    mixp[pl.ds(me, 1)] = mixed[pl.ds(me, 1)]

    up_copy.wait()
    for g in range(groups):
        ch = slice(g * group, (g + 1) * group)
        ug = upl[:, ch, :].reshape(long, width)
        gtok[g] = dot(block_diag(g), ug, 0, 0)
        prod = jnp.where(same, dot(ug, tokens[g], 1, 1), 0.0)
        wide = jnp.sum(prod.reshape(rows, group, long), axis=0)
        mix_out[g] = jnp.dot(wide, pick_f, precision=HIGH, preferred_element_type=F32)
        emb_up[ch, :] = jnp.sum(upl[:, ch, :].astype(F32), axis=0)

    def recv1(d, c):
        src = lax.rem(me + n - d, n)
        remote(mixed.at[src], mixp.at[src], s1, r1, d, src).wait_recv()
        return c

    lax.fori_loop(1, n, recv1, 0)
    w_copy.wait()

    x = mixp[...].reshape(chans, width).astype(F32)
    ir = lax.rsqrt(jnp.mean(x * x, axis=-1, keepdims=True) + 1e-06)
    inv[...] = ir
    gbs[...] = (x * ir * gain[...]).astype(BF16).reshape(n, cc, width)

    span = 512
    half = chans // 2

    def project(k, c):
        cols = pl.ds(pl.multiple_of(k * span, span), span)
        proj[:, cols] = dot(gbs[...].reshape(chans, width), w[:, cols]).astype(BF16)
        return c

    lax.fori_loop(0, 3 * width // span, project, 0)

    scale = 1.0 / math.sqrt(HDIM)
    fold = scale / math.log(2.0)

    def head_cols(h, part):
        return pl.ds(pl.multiple_of(part * width + h * HDIM, HDIM), HDIM)

    def forward(h, c):
        q, k, v = (proj[:, head_cols(h, part)] for part in range(3))
        s = dot(q, k, 1, 1)
        e = jnp.exp2((s - jnp.max(s, axis=-1, keepdims=True)) * fold)
        p = e * (1.0 / jnp.sum(e, axis=-1, keepdims=True))
        probs[pl.ds(h, 1)] = p[None]
        cols = head_cols(h, 0)
        att = dot(p.astype(BF16), v).astype(BF16)
        m = mixp[:, :, cols].astype(F32)
        encs[:, :, cols] = (m + att.reshape(n, cc, HDIM).astype(F32)).astype(BF16)
        return c

    lax.fori_loop(0, heads, forward, 0)

    def send3(d, c):
        peer = lax.rem(me + d, n)
        remote(encs.at[peer], enc_out.at[me, 0], s3, r3, d, peer).start()
        return c

    lax.fori_loop(1, n, send3, 0)
    own_enc = pltpu.make_async_copy(encs.at[me], enc_out.at[me, 0], lsem.at[3])
    own_enc.start()

    own_up.wait()

    def recv2(d, c):
        src = lax.rem(me + n - d, n)
        remote(up_hbm.at[src, 0], upp.at[src], s2, r2, d, src).wait_recv()
        return c

    lax.fori_loop(1, n, recv2, 0)

    def backward(h, c):
        q, k, v = (proj[:, head_cols(h, part)] for part in range(3))
        do = upp[:, :, head_cols(h, 0)].reshape(chans, HDIM)
        p = probs[pl.ds(h, 1)][0]
        dp = dot(do, v, 1, 1)
        gproj[:, head_cols(h, 2)] = dot(p.astype(BF16), do, 0, 0).astype(BF16)
        inner = jnp.sum(p * dp, axis=-1, keepdims=True)
        ds = (p * (dp - inner) * scale).astype(BF16)
        gproj[:, head_cols(h, 0)] = dot(ds, k).astype(BF16)
        gproj[:, head_cols(h, 1)] = dot(ds, q, 0, 0).astype(BF16)
        return c

    lax.fori_loop(0, heads, backward, 0)

    per = n // 2
    wide_cols = 256

    def finish(b, c):
        rs = pl.ds(pl.multiple_of(b * half, half), half)

        def back_project(k, c2):
            cols = pl.ds(pl.multiple_of(k * wide_cols, wide_cols), wide_cols)
            gn[:, cols] = dot(gproj[rs, :], w[cols, :], 1, 1)
            return c2

        lax.fori_loop(0, width // wide_cols, back_project, 0)
        scaled = gn[...] * gain[...]
        xb = mixp[pl.ds(b * per, per)].reshape(half, width).astype(F32)
        ib = inv[rs, :]
        mean = jnp.mean(scaled * xb, axis=-1, keepdims=True)
        gb = ib * (scaled - xb * ib * ib * mean)
        gbs[pl.ds(b * per, per)] = gb.astype(BF16).reshape(per, cc, width)

        def send4(j, c2):
            peer = b * per + j
            d = lax.rem(peer + n - me, n)

            @pl.when(peer != me)
            def _():
                remote(gbs.at[peer], gbr.at[me], s4, r4, d, peer).start()

            return c2

        lax.fori_loop(0, per, send4, 0)
        return c

    lax.fori_loop(0, 2, finish, 0)
    gbr[pl.ds(me, 1)] = gbs[pl.ds(me, 1)]

    def recv4(d, c):
        src = lax.rem(me + n - d, n)
        remote(gbs.at[src], gbr.at[src], s4, r4, d, src).wait_recv()
        return c

    lax.fori_loop(1, n, recv4, 0)

    for g in range(groups):
        ch = slice(g * group, (g + 1) * group)
        gb = gbr[:, ch, :]
        emb = emb_up[ch, :] + jnp.sum(gb.astype(F32), axis=0)
        emb_all[pl.ds(mypos, 1), ch, :] = emb[None]
        gg = gb.reshape(long, width)
        prod = jnp.where(same, dot(gg, tokens[g], 1, 1), 0.0)
        wide = jnp.sum(prod.reshape(rows, group, long), axis=0)
        mg = mix_out[g] + jnp.dot(wide, pick_f, precision=HIGH, preferred_element_type=F32)
        mg = jnp.concatenate([mg, jnp.zeros((group, 128 - group), F32)], axis=1)
        mix_all[pl.ds(mypos, 1), ch, :] = mg[None]

    def pos_copy(ref, ss, rs, q, slot, partner):
        return pltpu.make_async_remote_copy(
            src_ref=ref.at[slot], dst_ref=ref.at[slot], send_sem=ss.at[q], recv_sem=rs.at[q],
            device_id={"pos": partner},
        )

    def send_pos(q, c):
        partner = lax.rem(mypos + q, npos)
        pos_copy(emb_all, se, re, q, mypos, partner).start()
        pos_copy(mix_all, sm, rm, q, mypos, partner).start()
        return c

    lax.fori_loop(1, npos, send_pos, 0)

    for g in range(groups):
        ch = slice(g * group, (g + 1) * group)
        gg = gbr[:, ch, :].reshape(long, width)
        gt = (gtok[g] + dot(block_diag(g), gg, 0, 0)).astype(BF16)
        pg = patches[:, 0, ch, :].reshape(long, pix)
        tok_out[0, g] = dot(pg, gt, 0, 0)

    def recv_pos(q, c):
        src = lax.rem(mypos + npos - q, npos)
        pos_copy(emb_all, se, re, q, src, src).wait_recv()
        pos_copy(mix_all, sm, rm, q, src, src).wait_recv()
        return c

    lax.fori_loop(1, npos, recv_pos, 0)
    emb_out[...] = jnp.sum(emb_all[...], axis=0)
    mix_sum = jnp.sum(mix_all[...], axis=0)
    for g in range(groups):
        mix_out[g] = mix_sum[g * group:(g + 1) * group, :group]

    own_enc.wait()

    def drain(d, c):
        peer = lax.rem(me + d, n)
        src = lax.rem(me + n - d, n)
        remote(encs.at[src], enc_out.at[src, 0], s3, r3, d, src).wait_recv()
        remote(mixed.at[peer], mixp.at[me], s1, r1, d, peer).wait_send()
        remote(up_hbm.at[peer, 0], upp.at[me], s2, r2, d, peer).wait_send()
        remote(encs.at[peer], enc_out.at[me, 0], s3, r3, d, peer).wait_send()
        remote(gbs.at[peer], gbr.at[me], s4, r4, d, peer).wait_send()
        return c

    lax.fori_loop(1, n, drain, 0)

    def drain_pos(q, c):
        partner = lax.rem(mypos + q, npos)
        pos_copy(emb_all, se, re, q, mypos, partner).wait_send()
        pos_copy(mix_all, sm, rm, q, mypos, partner).wait_send()
        return c

    lax.fori_loop(1, npos, drain_pos, 0)


def local(n, npos, patches, tok_weight, mixing, chan_embed, norm_gain, qkv_weight, upstream):
    rows, _, cc, _ = patches.shape
    groups, pix, width = tok_weight.shape
    group = mixing.shape[1]
    chans = n * cc
    heads = width // HDIM
    vm = functools.partial(pl.BlockSpec, memory_space=pltpu.VMEM)
    anyspace = pl.BlockSpec(memory_space=pl.ANY)
    dma = pltpu.SemaphoreType.DMA
    out_shape = (
        jax.ShapeDtypeStruct((rows, 1, cc, width), BF16),
        jax.ShapeDtypeStruct((1, groups, pix, width), F32),
        jax.ShapeDtypeStruct((groups, group, group), F32),
        jax.ShapeDtypeStruct((cc, width), F32),
    )
    block = pltpu.VMEM((n, cc, width), BF16)
    scratch = [
        pltpu.VMEM((groups, rows * group, width), BF16),
        block, block, block, block,
        pltpu.VMEM(qkv_weight.shape, BF16),
        pltpu.VMEM((chans, 3 * width), BF16),
        pltpu.VMEM((heads, chans, chans), F32),
        pltpu.VMEM((chans, 1), F32),
        block,
        pltpu.VMEM((chans, 3 * width), BF16),
        pltpu.VMEM((chans // 2, width), F32),
        block, block,
        pltpu.VMEM((npos, cc, width), F32),
        pltpu.VMEM((npos, groups * group, 128), F32),
        pltpu.VMEM((groups, rows * group, width), F32),
        pltpu.VMEM((cc, width), F32),
    ] + [dma((n,))] * 8 + [dma((npos,))] * 4 + [dma((4,))]
    return pl.pallas_call(
        functools.partial(kernel, n, npos),
        out_shape=out_shape,
        in_specs=[vm()] * 5 + [anyspace] * 2,
        out_specs=(anyspace, vm(), vm(), vm()),
        scratch_shapes=scratch,
        compiler_params=pltpu.CompilerParams(
            collective_id=0, has_side_effects=True, vmem_limit_bytes=56 * 1024 * 1024
        ),
    )(patches, tok_weight, mixing, chan_embed, norm_gain.reshape(1, width), qkv_weight, upstream)


def solution(mesh):
    in_specs = (
        P(None, "pos", "chan", None),
        P("chan", None, None),
        P("chan", None, None),
        P("chan", None),
        P(),
        P(),
        P(None, "pos", "chan", None),
    )
    out_specs = (
        P(None, "pos", "chan", None),
        P("pos", "chan", None, None),
        P("chan", None, None),
        P("chan", None),
    )
    body = functools.partial(local, mesh.shape["chan"], mesh.shape["pos"])
    return jax.shard_map(body, mesh=mesh, in_specs=in_specs, out_specs=out_specs, check_vma=False)
```

profile of v0, /device:TPU:31, one launch (start us, length us, event | category | flops | bytes accessed | tf_op | source)
XLA Modules:
  0.0 111.5 jit_solution(5241549683898062764)
XLA Ops:
  0.6 105.8 %shard_map.102 = (bf16[16,1,32,1024]{3,2,1,0:T(8,128)(2,1)}, f32[1,2,256,1024]{3,2,1,0:T(8,128)}, f32[2,16,16]{2,1,0:T(8,128)}, f32[32,1024]{1,0:T(8,128)}) custom-call(bf16[16,1,32,256]{3,2,1,0:T(8,128)(2,1)} %patches.1, bf16[2,256,1024]{2,1,0:T(8,128)(2,1)} %tokw.1, bf16[2,16,16]{2,1,0:T(8,128)(2,1)} %mixing.1, bf16[32,1024]{1,0:T(8,128)(2,1)} %embed.1, ...), custom_call_target="tpu_custom_call" | custom-call | tf_op jit(solution)/shard_map/pallas_call | solution.py:328
  106.4 0.0 copy-start
  106.4 2.4 %copy.15 = bf16[16,1,32,1024]{3,2,1,0:T(8,128)(2,1)} copy(bf16[16,1,32,1024]{3,2,1,0:T(8,128)(2,1)} %get-tuple-element.8) | data formatting | bytes 2097152
  108.9 0.0 copy-done
  108.9 0.0 copy-start.2
  108.9 0.0 copy-start.1
  108.9 1.3 %copy.16 = f32[1,2,256,1024]{3,2,1,0:T(8,128)} copy(f32[1,2,256,1024]{3,2,1,0:T(8,128)S(1)} %copy-done) | data formatting | bytes 4194304
  110.2 0.0 copy-done.2
  110.2 0.6 copy.17
  110.8 0.0 copy-done.1
  110.8 0.7 copy.18
Async XLA Ops:
  106.4 2.4 %copy-start = (f32[1,2,256,1024]{3,2,1,0:T(8,128)S(1)}, f32[1,2,256,1024]{3,2,1,0:T(8,128)}, u32[]{:S(2)}) copy-start(f32[1,2,256,1024]{3,2,1,0:T(8,128)} %get-tuple-element.9) | copy-start | bytes 6291460
  108.9 1.3 %copy-start.2 = (f32[2,16,16]{2,1,0:T(8,128)S(1)}, f32[2,16,16]{2,1,0:T(8,128)}, u32[]{:S(2)}) copy-start(f32[2,16,16]{2,1,0:T(8,128)} %get-tuple-element.10) | copy-start | bytes 6148
  108.9 1.9 %copy-start.1 = (f32[32,1024]{1,0:T(8,128)S(1)}, f32[32,1024]{1,0:T(8,128)}, u32[]{:S(2)}) copy-start(f32[32,1024]{1,0:T(8,128)} %get-tuple-element.11) | copy-start | bytes 393220
where the time goes:
time: 112 us; the launch traced here: 111 us
  Pallas kernels  106 us (95%)
  local copies, waits for them, and re-layouts  5.03 us (4%)
    pallas_call x1, Pallas kernels, local(): pl.pallas_call(functools.partial(kernel, n, npos), out_shape=out_shape, i...  106 us
    unnamed x10, local copies, waits for them, and re-layouts  5.03 us

commit v1 on v0

--- a/solution.py
+++ b/solution.py
@@ -82,14 +82,16 @@
 
     pl.semaphore_wait(barrier, n - 1 + npos - 1)
 
-    def send1(d, c):
+    def send1(i, c):
+        d = n - i
         peer = lax.rem(me + d, n)
         remote(mixed.at[peer], mixp.at[me], s1, r1, d, peer).start()
         return c
 
     lax.fori_loop(1, n, send1, 0)
 
-    def send2(d, c):
+    def send2(i, c):
+        d = n - i
         peer = lax.rem(me + d, n)
         remote(up_hbm.at[peer, 0], upp.at[me], s2, r2, d, peer).start()
         return c
@@ -151,7 +153,8 @@
 
     lax.fori_loop(0, heads, forward, 0)
 
-    def send3(d, c):
+    def send3(i, c):
+        d = n - i
         peer = lax.rem(me + d, n)
         remote(encs.at[peer], enc_out.at[me, 0], s3, r3, d, peer).start()
         return c
@@ -186,7 +189,8 @@
     per = n // 2
     wide_cols = 256
 
-    def finish(b, c):
+    def finish(i, c):
+        b = lax.rem(me // per + 1 + i, 2)
         rs = pl.ds(pl.multiple_of(b * half, half), half)
 
         def back_project(k, c2):
@@ -203,7 +207,7 @@
         gbs[pl.ds(b * per, per)] = gb.astype(BF16).reshape(per, cc, width)
 
         def send4(j, c2):
-            peer = b * per + j
+            peer = b * per + lax.rem(me + n - j, per)
             d = lax.rem(peer + n - me, n)
 
             @pl.when(peer != me)

time: 112 us -> 109 us (0.973)
  the two profiles are of different devices: /device:TPU:31 before, /device:TPU:2 now
where the time goes in v1:
time: 109 us
  Pallas kernels  103 us (94%)
  local copies, waits for them, and re-layouts  5.03 us (5%)
    pallas_call x1, Pallas kernels, local(): pl.pallas_call(functools.partial(kernel, n, npos), out_shape=out_shape, i...  103 us
    unnamed x10, local copies, waits for them, and re-layouts  5.03 us

profile of v1, /device:TPU:2, one launch (start us, length us, event | category | flops | bytes accessed | tf_op | source)
XLA Modules:
  0.0 109.0 jit_solution(14899213340871028257)
XLA Ops:
  0.6 103.3 %shard_map.102 = (bf16[16,1,32,1024]{3,2,1,0:T(8,128)(2,1)}, f32[1,2,256,1024]{3,2,1,0:T(8,128)}, f32[2,16,16]{2,1,0:T(8,128)}, f32[32,1024]{1,0:T(8,128)}) custom-call(bf16[16,1,32,256]{3,2,1,0:T(8,128)(2,1)} %patches.1, bf16[2,256,1024]{2,1,0:T(8,128)(2,1)} %tokw.1, bf16[2,16,16]{2,1,0:T(8,128)(2,1)} %mixing.1, bf16[32,1024]{1,0:T(8,128)(2,1)} %embed.1, ...), custom_call_target="tpu_custom_call" | custom-call | tf_op jit(solution)/shard_map/pallas_call | solution.py:332
  103.9 0.0 copy-start
  103.9 2.4 %copy.15 = bf16[16,1,32,1024]{3,2,1,0:T(8,128)(2,1)} copy(bf16[16,1,32,1024]{3,2,1,0:T(8,128)(2,1)} %get-tuple-element.8) | data formatting | bytes 2097152
  106.4 0.0 copy-done
  106.4 0.0 copy-start.2
  106.4 0.0 copy-start.1
  106.4 1.3 %copy.16 = f32[1,2,256,1024]{3,2,1,0:T(8,128)} copy(f32[1,2,256,1024]{3,2,1,0:T(8,128)S(1)} %copy-done) | data formatting | bytes 4194304
  107.7 0.0 copy-done.2
  107.7 0.6 copy.17
  108.3 0.0 copy-done.1
  108.3 0.7 copy.18
Async XLA Ops:
  103.9 2.4 %copy-start = (f32[1,2,256,1024]{3,2,1,0:T(8,128)S(1)}, f32[1,2,256,1024]{3,2,1,0:T(8,128)}, u32[]{:S(2)}) copy-start(f32[1,2,256,1024]{3,2,1,0:T(8,128)} %get-tuple-element.9) | copy-start | bytes 6291460
  106.4 1.3 %copy-start.2 = (f32[2,16,16]{2,1,0:T(8,128)S(1)}, f32[2,16,16]{2,1,0:T(8,128)}, u32[]{:S(2)}) copy-start(f32[2,16,16]{2,1,0:T(8,128)} %get-tuple-element.10) | copy-start | bytes 6148
  106.4 1.9 %copy-start.1 = (f32[32,1024]{1,0:T(8,128)S(1)}, f32[32,1024]{1,0:T(8,128)}, u32[]{:S(2)}) copy-start(f32[32,1024]{1,0:T(8,128)} %get-tuple-element.11) | copy-start | bytes 393220
